TPU v7x, 32 devices: a whole 2x2x4 slice. The times are simulated.
32 devices in a mesh: grp: 2 (over y), seq: 4 (over z), head: 2 (over x), rep: 2 (over core).
Axes of the slice: x: 2, y: 2, z: 4, core: 2. Of those that a mesh axis runs over, the one named last changes fastest.
Arguments:
- latents: bfloat16 [2048, 1024], P(('grp', 'seq', 'rep')), parts along dimension 0, may hold values from -6 to 6
- cotangent: bfloat16 [2048, 1024], P(('grp', 'seq', 'rep')), parts along dimension 0, may hold values from -12 to 12
- tokens: bfloat16 [4096, 1024], P(('grp', 'seq', 'rep')), parts along dimension 0, may hold values from -200 to 200
- counts: int32 [16], P(('grp', 'seq', 'rep')), parts along dimension 0, may hold values from 1 to 256, 1280 in all
- w_query: bfloat16 [1024, 1024], P(None, 'head'), may hold values from -0.1875 to 0.1875
- w_key: bfloat16 [1024, 1024], P(None, 'head'), may hold values from -0.1875 to 0.1875
- w_value: bfloat16 [1024, 1024], P(None, 'head'), may hold values from -0.1875 to 0.1875
- w_out: bfloat16 [1024, 1024], P('head'), may hold values from -0.1875 to 0.1875
Outputs:
- attended: bfloat16 [2048, 1024], P(('grp', 'seq', 'rep'), 'head'), parts along dimension 0
- latent_grad: bfloat16 [2048, 1024], P(('grp', 'seq', 'rep'), 'head'), parts along dimension 0
- token_grad: bfloat16 [4096, 1024], P(('grp', 'seq', 'rep'), 'head'), parts along dimension 0
There are 2 independent parts, one for each index of `grp`. A program takes and returns all parts, laid end to end along the dimension named above; an argument that names none is the same for every part. Nothing has to cross between parts.
Inputs may be any that keep to these rules, and one draw needn't show every extreme that they name: The counts of a group sum to 1280; the largest equals 256.
All inputs are finite; a program needn't handle non-finite values.
Results may differ from a plain program's by a relative error of at most 0.039.
The roundings to bfloat16 on the way count: a program that leaves them out, or rounds other values in their place, can miss the bound.
Values may be sent and summed in bfloat16 or wider, within the bound.
A program may use at most 128 MiB of HBM per device.

v0:
```python
import jax
import jax.numpy as jnp
from jax import lax
from jax.sharding import PartitionSpec as P

D = 1024
HEADS = 16


def combined_all(value, axis, join):
    pieces = jax.tree.map(lambda part: lax.all_gather(part, axis), value)
    head = jax.tree.map(lambda part: part[0], pieces)
    tail = jax.tree.map(lambda part: part[1:], pieces)
    running, _ = lax.scan(lambda running, slab: (join(running, slab), None), head, tail)
    return running


def merge_parts(earlier, latter):
    high_first, sums_first, accum_first = earlier
    high_second, sums_second, accum_second = latter
    highest = jnp.maximum(high_first, high_second)
    factor_first = jnp.exp(high_first - highest)
    factor_second = jnp.exp(high_second - highest)
    repeats = accum_first.shape[-1] // high_first.shape[-1]
    merged = accum_first * jnp.repeat(factor_first, repeats, axis=-1) + accum_second * jnp.repeat(
        factor_second, repeats, axis=-1
    )
    return (highest, sums_first * factor_first + sums_second * factor_second, merged)


def head_major(matrix, heads_here):
    rows_count = matrix.shape[0]
    return matrix.reshape(rows_count, heads_here, matrix.shape[1] // heads_here).transpose(1, 0, 2)


def row_major(stacked):
    return stacked.transpose(1, 0, 2).reshape(stacked.shape[1], stacked.shape[0] * stacked.shape[2])


def contract_last(left, right):
    return lax.dot_general(
        left, right, (((1,), (1,)), ((), ())), preferred_element_type=jnp.float32
    )


def contract_first(left, right):
    return lax.dot_general(
        left, right, (((0,), (0,)), ((), ())), preferred_element_type=jnp.float32
    )


def on_device(latents, cotangent, tokens, counts, w_query, w_key, w_value, w_out):
    columns = w_query.shape[1]
    head_size = D // HEADS
    heads_here = columns // head_size
    scale = head_size ** (-0.5)
    lat_rows = latents.shape[0]
    row_start = lax.axis_index(("seq", "rep")) * lat_rows
    query_rows = jnp.dot(latents, w_query, preferred_element_type=jnp.float32).astype(jnp.bfloat16)
    grad_rows = contract_last(cotangent, w_out).astype(jnp.bfloat16)
    queries, grad_att = (
        lax.all_gather(query_rows, ("seq", "rep"), axis=0, tiled=True),
        lax.all_gather(grad_rows, ("seq", "rep"), axis=0, tiled=True),
    )
    key_rows = jnp.dot(tokens, w_key, preferred_element_type=jnp.float32).astype(jnp.bfloat16)
    value_rows = jnp.dot(tokens, w_value, preferred_element_type=jnp.float32).astype(jnp.bfloat16)
    live_mask = jnp.arange(tokens.shape[0], dtype=jnp.int32) < counts[0]
    query_heads = head_major(queries, heads_here)
    grad_heads = head_major(grad_att, heads_here)
    key_heads = head_major(key_rows, heads_here)
    value_heads = head_major(value_rows, heads_here)

    def masked_scores(query_head, key_head):
        scores = contract_last(query_head, key_head) * scale
        return jnp.where(live_mask[None, :], scores, -jnp.inf)

    def forward_head(operands):
        query_head, key_head, value_head = operands
        scores = masked_scores(query_head, key_head)
        highest = jnp.max(scores, axis=1)
        expo = jnp.exp(scores - highest[:, None])
        weighted = jnp.dot(
            expo.astype(jnp.bfloat16), value_head, preferred_element_type=jnp.float32
        )
        return (highest, jnp.sum(expo, axis=1), weighted)

    highs, sums, accums = lax.map(forward_head, (query_heads, key_heads, value_heads))
    highs = highs.T
    sums = sums.T
    accums = row_major(accums)
    highest, denominator, numerator = combined_all(
        (highs, sums, accums), ("seq", "rep"), merge_parts
    )
    attention = (numerator / jnp.repeat(denominator, head_size, axis=1)).astype(jnp.bfloat16)
    log_norms = highest + jnp.log(denominator)
    all_rows = attention.shape[0]
    row_terms = jnp.sum(
        (attention.astype(jnp.float32) * grad_att.astype(jnp.float32)).reshape(
            all_rows, heads_here, head_size
        ),
        axis=2,
    )
    attended_rows = lax.dynamic_slice_in_dim(attention, row_start, lat_rows, 0)
    out_terms = jnp.dot(attended_rows, w_out, preferred_element_type=jnp.float32)
    attended = lax.psum_scatter(
        out_terms.astype(jnp.bfloat16), "head", scatter_dimension=1, tiled=True
    )

    def backward_head(operands):
        query_head, key_head, value_head, grad_head, log_norm, row_term = operands
        scores = masked_scores(query_head, key_head)
        weights = jnp.exp(scores - log_norm[:, None])
        grad_value = contract_first(weights.astype(jnp.bfloat16), grad_head).astype(jnp.bfloat16)
        grad_weights = contract_last(grad_head, value_head)
        grad_scores = (weights * (grad_weights - row_term[:, None]) * scale).astype(jnp.bfloat16)
        query_term = jnp.dot(grad_scores, key_head, preferred_element_type=jnp.float32)
        grad_key = contract_first(grad_scores, query_head).astype(jnp.bfloat16)
        return (query_term, grad_key, grad_value)

    query_terms, grad_keys, grad_values = lax.map(
        backward_head, (query_heads, key_heads, value_heads, grad_heads, log_norms.T, row_terms.T)
    )
    query_terms = row_major(query_terms)
    query_total = lax.psum(query_terms, ("seq", "rep"))
    query_grad = lax.dynamic_slice_in_dim(query_total, row_start, lat_rows, 0)
    latent_terms = contract_last(query_grad.astype(jnp.bfloat16), w_query)
    latent_grad = lax.psum_scatter(latent_terms, "head", scatter_dimension=1, tiled=True).astype(
        jnp.bfloat16
    )
    token_terms = contract_last(row_major(grad_keys), w_key) + contract_last(
        row_major(grad_values), w_value
    )
    token_grad = lax.psum_scatter(
        token_terms.astype(jnp.bfloat16), "head", scatter_dimension=1, tiled=True
    )
    return (attended, latent_grad, token_grad)


def solution(mesh):
    in_specs = (
        P(("grp", "seq", "rep"), None),
        P(("grp", "seq", "rep"), None),
        P(("grp", "seq", "rep"), None),
        P(("grp", "seq", "rep")),
        P(None, "head"),
        P(None, "head"),
        P(None, "head"),
        P("head", None),
    )
    out_specs = (
        P(("grp", "seq", "rep"), "head"),
        P(("grp", "seq", "rep"), "head"),
        P(("grp", "seq", "rep"), "head"),
    )
    return jax.shard_map(
        on_device, mesh=mesh, in_specs=in_specs, out_specs=out_specs, check_vma=False
    )
```

profile of v0, /device:TPU:0, one launch (start us, length us, event | category | flops | bytes accessed | tf_op | source)
XLA Modules:
  0.0 508.8 jit_solution(16419947829245512291)
XLA Ops:
  7.2 2.4 convolution_convert_fusion.6
  9.7 2.5 convolution_convert_fusion.5
  15.6 19.5 %all-gather.6.cloned.1.call-done = bf16[1024,512]{1,0:T(8,128)(2,1)} async-done(((bf16[128,512]{1,0:T(8,128)(2,1)}), bf16[1024,512]{1,0:T(8,128)(2,1)}) %all-gather.6.cloned.1.call-update) | async-done | bytes 1048592 | tf_op jit(solution)/shard_map/all_gather | solution.py:62
  40.9 32.7 %while.45 = (s32[]{:T(128)}, f32[8,1024]{1,0:T(8,128)S(1)}, f32[8,1024]{1,0:T(8,128)S(1)}, f32[8,1024,64]{1,2,0:T(8,128)}, bf16[8,1024,64]{2,1,0:T(8,128)(2,1)S(...) while((s32[]{:T(128)}, f32[8,1024]{1,0:T(8,128)S(1)}, ...), condition=%wide.region_3.4_spmd.clone, body=%wide.region_0.3_spmd.clone.sunk | while | flops 68942080 | bytes 3836785 | solution.py:87
  73.6 3.7 copy.56
  77.4 14.2 %all-gather = f32[8192,8]{0,1:T(8,128)S(1)} all-gather(f32[1024,8]{0,1:T(8,128)S(1)} %bitcast.189), channel_id=2, replica_groups=mesh['grp'=2,'seq'=4,'head'=2,'rep'=2] {'seq','rep'}, dimensions={0}, use_global_device_ids=true | all-gather | bytes 294912 | tf_op jit(solution)/shard_map/all_gather | solution.py:11
  91.7 16.4 %all-gather.1 = f32[8192,8]{0,1:T(8,128)S(1)} all-gather(f32[1024,8]{0,1:T(8,128)S(1)} %bitcast.190), channel_id=3, replica_groups=mesh['grp'=2,'seq'=4,'head'=2,'rep'=2] {'seq','rep'}, dimensions={0}, use_global_device_ids=true | all-gather | bytes 294912 | tf_op jit(solution)/shard_map/all_gather | solution.py:11
  111.1 119.2 %all-gather.8.cloned.1.call-done = f32[8,1024,512]{2,1,0:T(8,128)} async-done(((f32[1,1024,512]{2,1,0:T(8,128)}), f32[8,1024,512]{2,1,0:T(8,128)}) %all-gather.8.cloned.1.call-update) | async-done | bytes 16777232 | tf_op jit(solution)/shard_map/all_gather | solution.py:11
  233.9 13.0 %slice.33 = f32[7,1024,512]{2,1,0:T(8,128)} slice(f32[8,1024,512]{2,1,0:T(8,128)} %all-gather.8.cloned.1.call-done), slice={[1:8], [0:1024], [0:512]} | slice | bytes 29360128 | tf_op jit(solution)/shard_map/slice | solution.py:13
  246.9 64.6 %while.44 = (s32[]{:T(128)}, f32[1024,8]{0,1:T(8,128)S(1)}, f32[1024,8]{0,1:T(8,128)S(1)}, f32[1024,512]{0,1:T(8,128)}, f32[7,1024,8]{1,2,0:T(8,128)S(1)}, /*ind...) while((s32[]{:T(128)}, f32[1024,8]{0,1:T(8,128)S(1)}, f32[1024,8]{0,1:T(8,128)S(1)}, ...), condition=%wide.region_5.6_spmd, body=%wide.region_4.5_spmd.sunk | while | flops 1622018 | bytes 15007837 | solution.py:14
  247.7 3.1 constant_dynamic-slice_fusion.5
  252.8 3.4 fusion.99
  257.0 3.1 constant_dynamic-slice_fusion.5
  262.0 3.4 fusion.99
  266.2 3.1 constant_dynamic-slice_fusion.5
  271.2 3.4 fusion.99
  275.4 3.1 constant_dynamic-slice_fusion.5
  280.5 3.4 fusion.99
  284.7 3.1 constant_dynamic-slice_fusion.5
  289.7 3.4 fusion.99
  293.9 3.1 constant_dynamic-slice_fusion.5
  298.9 3.4 fusion.99
  303.1 3.1 constant_dynamic-slice_fusion.5
  308.2 3.4 fusion.99
  313.1 3.1 copy.60
  318.0 4.8 convert_multiply_fusion
  325.9 64.6 %while.46 = (s32[]{:T(128)}, f32[8,1024,64]{1,2,0:T(8,128)S(1)}, bf16[8,256,64]{1,2,0:T(8,128)(2,1)S(1)}, bf16[8,256,64]{1,2,0:T(8,128)(2,1)}, bf16[8,1024,64]{2...) while((s32[]{:T(128)}, f32[8,1024,64]{1,2,0:T(8,128)S(1)}, ...), condition=%wide.region_9.10_spmd.clone, body=%wide.region_8.9_spmd.clone.sunk | while | flops 169902336 | bytes 6059645 | solution.py:120
  390.6 62.7 %all-reduce.1 = bf16[1024,512]{0,1:T(8,128)(2,1)} all-reduce(f32[1024,512]{0,1:T(8,128)S(1)} %bitcast.175), channel_id=1, replica_groups=mesh['grp'=2,'seq'=4,'head'=2,'rep'=2] {'seq','rep'}, use_global_device_ids=true, to_apply=%region_10.11 | all-reduce | flops 524288 | bytes 3145728 | tf_op jit(solution)/shard_map/psum | solution.py:124
  453.2 2.7 fusion.53
  460.9 9.4 %reduce-scatter.6.cloned.1.call-done = f32[128,512]{1,0:T(8,128)} async-done(((f32[128,1024]{1,0:T(8,128)}), f32[128,512]{1,0:T(8,128)}) %reduce-scatter.6.cloned.1.call-update) | async-done | bytes 262160 | tf_op jit(solution)/shard_map/reduce_scatter | solution.py:127
  471.9 12.8 %reduce-scatter.4.cloned.1.call-done = bf16[128,512]{1,0:T(8,128)(2,1)} async-done(((bf16[128,1024]{1,0:T(8,128)(2,1)}), bf16[128,512]{1,0:T(8,128)(2,1)}) %reduce-scatter.4.cloned.1.call-update) | async-done | bytes 131088 | tf_op jit(solution)/shard_map/reduce_scatter | solution.py:105
  484.7 17.3 %reduce-scatter.8.cloned.1.call-done = bf16[256,512]{1,0:T(8,128)(2,1)} async-done(((bf16[256,1024]{1,0:T(8,128)(2,1)}), bf16[256,512]{1,0:T(8,128)(2,1)}) %reduce-scatter.8.cloned.1.call-update) | async-done | bytes 262160 | tf_op jit(solution)/shard_map/reduce_scatter | solution.py:133
  (177 shorter events, 144.6 us)
Async XLA Ops:
  7.2 5.2 %copy-start = (bf16[1024,512]{1,0:T(8,128)(2,1)S(1)}, bf16[1024,512]{1,0:T(8,128)(2,1)}, u32[]{:S(2)}) copy-start(bf16[1024,512]{1,0:T(8,128)(2,1)} %param.19) | copy-start | bytes 3145732
  7.2 5.2 %copy-start.6 = (bf16[256,1024]{1,0:T(8,128)(2,1)S(1)}, bf16[256,1024]{1,0:T(8,128)(2,1)}, u32[]{:S(2)}) copy-start(bf16[256,1024]{1,0:T(8,128)(2,1)} %param.16) | copy-start | bytes 1572868
  7.2 27.9 %all-gather.6.cloned.1.call-start = ((), (), s32[]{:S(2)}) async-start(), calls=%async_computation.3 | async-start | bytes 1179648 | tf_op jit(solution)/shard_map/all_gather | solution.py:62
  9.6 4.3 copy-start.4
  9.7 99.1 %all-gather.10.cloned.1.call-start = ((), (), s32[]{:S(2)}) async-start(), calls=%async_computation.6 | async-start | bytes 1179648 | tf_op jit(solution)/shard_map/all_gather | solution.py:63
  12.3 218.0 %all-gather.8.cloned.1.call-start = ((), (), s32[]{:S(2)}) async-start(), calls=%async_computation.4 | async-start | bytes 18874368 | tf_op jit(solution)/shard_map/all_gather | solution.py:11
  73.6 3.7 copy-start.2
  77.3 393.0 %reduce-scatter.6.cloned.1.call-start = ((), (), s32[]{:S(2)}) async-start(), calls=%async_computation.7 | async-start | bytes 786432 | tf_op jit(solution)/shard_map/reduce_scatter | solution.py:127
  313.1 3.1 copy-start.1
  324.8 1.1 copy-start.7
  453.2 2.8 copy-start.3
  455.9 2.7 copy-start.5
  455.9 28.8 %reduce-scatter.4.cloned.1.call-start = ((), (), s32[]{:S(2)}) async-start(), calls=%async_computation.5 | async-start | bytes 393216 | tf_op jit(solution)/shard_map/reduce_scatter | solution.py:105
  458.0 43.9 %reduce-scatter.8.cloned.1.call-start = ((), (), s32[]{:S(2)}) async-start(), calls=%async_computation.8 | async-start | bytes 786432 | tf_op jit(solution)/shard_map/reduce_scatter | solution.py:133
Sparse Core Ops, SparseCore 0:
  10.2 24.8 all-gather.5
  37.2 21.7 all-gather.9
  77.5 152.7 all-gather.7
  456.1 14.2 reduce-scatter.5
  473.0 11.6 reduce-scatter.3
  487.4 14.5 reduce-scatter.7
where the time goes:
time: 513 us; the launch traced here: 509 us
  waiting for transfers between devices  178 us (35%)
  blocking collectives  93.3 us (18%)
  matrix products  90.3 us (18%)
  local copies, waits for them, and re-layouts  83.2 us (16%)
  other arithmetic  48.5 us (9%)
  between operations  14.3 us (3%)
    all_gather x1, waiting for transfers between devices, combined_all(): pieces = jax.tree.map(lambda part: lax.all_gather(part, axis), value)  119 us
    psum x1, blocking collectives, on_device(): query_total = lax.psum(query_terms, ('seq', 'rep'))  62.7 us
    dot_general x28, matrix products, contract_last(): lax.dot_general(left, right, (((1,), (1,)), ((), ())), preferred_element_...  37.8 us
    dynamic_slice x14, local copies, waits for them, and re-layouts, combined_all(): lax.scan(lambda running, slab: (join(running, slab), None), head, tail)  35.1 us
    all_gather x2, blocking collectives, combined_all(): pieces = jax.tree.map(lambda part: lax.all_gather(part, axis), value)  30.6 us
    add x7, other arithmetic, merge_parts(): accum_first * jnp.repeat(factor_first, repeats, axis=-1)  23.9 us
    dot_general x16, matrix products, contract_first(): lax.dot_general(left, right, (((0,), (0,)), ((), ())), preferred_element_...  23.4 us
    all_gather x1, waiting for transfers between devices, on_device(): lax.all_gather(query_rows, ('seq', 'rep'), axis=0, tiled=True)  19.5 us
  transfers between devices with their start and end apart: 6, of which 5 were waited for; matrix products, arithmetic and copies ran while one was open for 11% of the time, Pallas kernels for 0%

commit v1 on v0

--- a/solution.py
+++ b/solution.py
@@ -1,6 +1,10 @@
+import functools
+
 import jax
 import jax.numpy as jnp
 from jax import lax
+from jax.experimental import pallas as pl
+from jax.experimental.pallas import tpu as pltpu
 from jax.sharding import PartitionSpec as P
 
 D = 1024
@@ -136,6 +140,312 @@
     return (attended, latent_grad, token_grad)
 
 
+MESH = pl.DeviceIdType.MESH
+BF = jnp.bfloat16
+F32 = jnp.float32
+
+
+def remote(src, dst, send, recv, device):
+    return pltpu.make_async_remote_copy(
+        src_ref=src, dst_ref=dst, send_sem=send, recv_sem=recv, device_id=device, device_id_type=MESH
+    )
+
+
+def fused_kernel(
+    n_seq, n_head, n_rep,
+    latents, cotangent, tokens, counts, w_query, w_key, w_value, w_out,
+    attended, latent_grad, token_grad,
+    q_all, g_all, g_t, k_all, v_all, k_t, v_t, bias, expo, highs,
+    acc_send, acc_recv, st_send, st_recv, norm_row, dq_send, dq_recv, dk, dv, dkv_send, dkv_recv,
+    att_stage, att_recv, lat_stage, lat_recv, tok_stage, tok_recv,
+    z_send, z_recv, r_send, r_recv, h_send, h_recv,
+):
+    lat, tok, cols = latents.shape[0], tokens.shape[0], w_query.shape[1]
+    hd = D // HEADS
+    wide = 2 * hd
+    pairs = cols // wide
+    scale = hd ** (-0.5)
+    z, h, r = lax.axis_index("seq"), lax.axis_index("head"), lax.axis_index("rep")
+    other = 1 - r
+
+    def zp(k):
+        return lax.rem(z + k, n_seq)
+
+    def hp(k):
+        return lax.rem(h + k, n_head)
+
+    barrier = pltpu.get_barrier_semaphore()
+    for k in range(1, n_seq):
+        pl.semaphore_signal(barrier, inc=1, device_id={"seq": zp(k)}, device_id_type=MESH)
+    for k in range(1, n_head):
+        pl.semaphore_signal(barrier, inc=1, device_id={"head": hp(k)}, device_id_type=MESH)
+    pl.semaphore_signal(barrier, inc=1, device_id={"rep": other}, device_id_type=MESH)
+
+    def z_copy(kind, src, dst, peer, slot_send, slot_recv):
+        return remote(src, dst, z_send.at[kind, slot_send], z_recv.at[kind, slot_recv], {"seq": peer})
+
+    def q_copy(peer, owner):
+        return z_copy(0, q_all.at[owner], q_all.at[owner], peer, peer, owner)
+
+    def g_copy(peer, owner):
+        return z_copy(1, g_all.at[owner], g_all.at[owner], peer, peer, owner)
+
+    def acc_copy(peer, sender):
+        return z_copy(2, acc_send.at[peer], acc_recv.at[sender], peer, peer, sender)
+
+    def st_copy(peer, sender):
+        return z_copy(3, st_send.at[peer], st_recv.at[sender], peer, peer, sender)
+
+    def norm_copy(peer, owner):
+        return z_copy(4, norm_row.at[owner], norm_row.at[owner], peer, peer, owner)
+
+    def dq_copy(peer, sender):
+        return z_copy(5, dq_send.at[peer], dq_recv.at[sender], peer, peer, sender)
+
+    def r_copy(index, src, dst):
+        return remote(src, dst, r_send.at[index], r_recv.at[index], {"rep": other})
+
+    own, theirs = pl.ds(0, tok), pl.ds(tok, tok)
+    k_copy = r_copy(0, k_all.at[own], k_all.at[theirs])
+    v_copy = r_copy(1, v_all.at[own], v_all.at[theirs])
+    b_copy = r_copy(2, bias.at[own], bias.at[theirs])
+    dkv_copy = r_copy(3, dkv_send, dkv_recv)
+
+    def h_copy(index, stage, landing, peer, sender):
+        return remote(
+            stage.at[peer], landing.at[sender], h_send.at[index, peer], h_recv.at[index, sender], {"head": peer}
+        )
+
+    q_all[z] = (jnp.dot(latents[...], w_query[...], preferred_element_type=F32).astype(BF) * scale).astype(BF)
+    pl.semaphore_wait(barrier, n_seq - 1 + n_head - 1 + 1)
+    for k in range(1, n_seq):
+        q_copy(zp(k), z).start()
+    k_all[own, :] = jnp.dot(tokens[...], w_key[...], preferred_element_type=F32).astype(BF)
+    k_copy.start()
+    rows = lax.broadcasted_iota(jnp.int32, (tok, 128), 0)
+    bias[own, :] = jnp.where(rows < counts[0], 0.0, -jnp.inf).astype(F32)
+    b_copy.start()
+    v_all[own, :] = jnp.dot(tokens[...], w_value[...], preferred_element_type=F32).astype(BF)
+    v_copy.start()
+    grads = contract_last(cotangent[...], w_out[...])
+    g_all[z] = grads.astype(BF)
+    for k in range(1, n_seq):
+        g_copy(zp(k), z).start()
+    g_t[...] = grads.T.astype(BF)
+    k_t[:, 0:tok] = k_all[own, :].astype(F32).T.astype(BF)
+    v_t[:, 0:tok] = v_all[own, :].astype(F32).T.astype(BF)
+    k_copy.wait_recv()
+    k_t[:, tok:2 * tok] = k_all[theirs, :].astype(F32).T.astype(BF)
+    b_copy.wait_recv()
+    v_copy.wait_recv()
+    v_t[:, tok:2 * tok] = v_all[theirs, :].astype(F32).T.astype(BF)
+
+    lane = lax.broadcasted_iota(jnp.int32, (lat, wide), 1)
+    upper = lax.broadcasted_iota(jnp.int32, (wide, lat), 0)
+
+    def stacked(block):
+        zero = jnp.zeros_like(block)
+        return jnp.concatenate([jnp.where(lane < hd, block, zero), jnp.where(lane < hd, zero, block)], axis=0)
+
+    def halves(both):
+        return jnp.where(upper < hd, both[:, :lat], both[:, lat:])
+
+    def forward(j, acc_out, stat_out):
+        for p in range(pairs):
+            span = slice(p * wide, (p + 1) * wide)
+            qs = stacked(q_all[j, :, span])
+            live = bias[...]
+            scores = contract_last(k_all[:, span], qs)
+            scores = scores + jnp.concatenate([live] * (2 * lat // 128), axis=1)
+            high = jnp.max(scores, axis=0, keepdims=True)
+            e = jnp.exp(scores - high)
+            expo[j, p] = e
+            highs[j, p] = high
+            stat_out[p, 0:1, :] = high
+            stat_out[p, 1:2, :] = jnp.sum(e, axis=0, keepdims=True)
+            out = jnp.dot(v_t[span, :], e.astype(BF), preferred_element_type=F32)
+            acc_out[span, :] = halves(out).astype(BF)
+
+    forward(z, acc_recv.at[z], st_recv.at[z])
+
+    def forward_step(k, carry):
+        j = zp(k)
+        q_copy(j, j).wait_recv()
+        forward(j, acc_send.at[j], st_send.at[j])
+        acc_copy(j, z).start()
+        st_copy(j, z).start()
+        return carry
+
+    lax.fori_loop(1, n_seq, forward_step, 0)
+
+    for k in range(1, n_seq):
+        acc_copy(zp(k), zp(k)).wait_recv()
+        st_copy(zp(k), zp(k)).wait_recv()
+
+    att_rows = []
+    for p in range(pairs):
+        span = slice(p * wide, (p + 1) * wide)
+        highest = st_recv[0, p, 0:1, :]
+        for s in range(1, n_seq):
+            highest = jnp.maximum(highest, st_recv[s, p, 0:1, :])
+        total = jnp.zeros_like(highest)
+        numerator = jnp.zeros((wide, lat), F32)
+        for s in range(n_seq):
+            factor = jnp.exp(st_recv[s, p, 0:1, :] - highest)
+            total = total + st_recv[s, p, 1:2, :] * factor
+            spread = jnp.where(upper < hd, factor[:, :lat], factor[:, lat:])
+            numerator = numerator + acc_recv[s, span, :].astype(F32) * spread
+        below = jnp.where(upper < hd, total[:, :lat], total[:, lat:])
+        att = (numerator / below).astype(BF).astype(F32)
+        att_rows.append(att)
+        product = att * g_t[span, :].astype(F32)
+        norm_row[z, p, 0:1, :] = highest + jnp.log(total)
+        norm_row[z, p, 1:2, :] = jnp.concatenate(
+            [jnp.sum(product[:hd], axis=0, keepdims=True), jnp.sum(product[hd:], axis=0, keepdims=True)], axis=1
+        )
+    for k in range(1, n_seq):
+        norm_copy(zp(k), z).start()
+
+    def stage_columns(stage, terms):
+        for g in range(n_head):
+            stage[g] = terms[:, g * cols:(g + 1) * cols].astype(BF)
+
+    attention = jnp.concatenate([part.T for part in att_rows], axis=1).astype(BF)
+    stage_columns(att_stage, jnp.dot(attention, w_out[...], preferred_element_type=F32))
+    for k in range(1, n_head):
+        h_copy(0, att_stage, att_recv, hp(k), h).start()
+
+    dk[...] = jnp.zeros_like(dk)
+    dv[...] = jnp.zeros_like(dv)
+
+    def backward(j, dq_out):
+        for p in range(pairs):
+            span = slice(p * wide, (p + 1) * wide)
+            qs = stacked(q_all[j, :, span])
+            gs = stacked(g_all[j, :, span])
+            weights = expo[j, p] * jnp.exp(highs[j, p] - norm_row[j, p, 0:1, :])
+            dv[:, span] += jnp.dot(weights.astype(BF), gs, preferred_element_type=F32)
+            inner = contract_last(v_all[:, span], gs)
+            ds = (weights * (inner - norm_row[j, p, 1:2, :])).astype(BF)
+            dk[:, span] += jnp.dot(ds, qs, preferred_element_type=F32)
+            both = jnp.dot(k_t[span, :], ds, preferred_element_type=F32)
+            dq_out[span, :] = (halves(both) * scale).astype(BF)
+
+    backward(z, dq_recv.at[z])
+
+    def backward_step(k, carry):
+        j = zp(k)
+        g_copy(j, j).wait_recv()
+        norm_copy(j, j).wait_recv()
+        backward(j, dq_send.at[j])
+        dq_copy(j, z).start()
+        return carry
+
+    lax.fori_loop(1, n_seq, backward_step, 0)
+
+    dkv_send[0] = dk[theirs, :].astype(BF)
+    dkv_send[1] = dv[theirs, :].astype(BF)
+    dkv_copy.start()
+
+    dkv_copy.wait_recv()
+    grad_key = (dk[own, :] + dkv_recv[0].astype(F32)).astype(BF)
+    grad_value = (dv[own, :] + dkv_recv[1].astype(F32)).astype(BF)
+    stage_columns(tok_stage, contract_last(grad_key, w_key[...]) + contract_last(grad_value, w_value[...]))
+    for k in range(1, n_head):
+        h_copy(1, tok_stage, tok_recv, hp(k), h).start()
+
+    for k in range(1, n_seq):
+        dq_copy(zp(k), zp(k)).wait_recv()
+    total_t = dq_recv[0].astype(F32)
+    for s in range(1, n_seq):
+        total_t = total_t + dq_recv[s].astype(F32)
+    stage_columns(lat_stage, contract_last(total_t.T.astype(BF), w_query[...]))
+    for k in range(1, n_head):
+        h_copy(2, lat_stage, lat_recv, hp(k), h).start()
+
+    def summed(index, stage, landing, out):
+        total = stage[h].astype(F32)
+        for k in range(1, n_head):
+            h_copy(index, stage, landing, hp(k), hp(k)).wait_recv()
+            total = total + landing[hp(k)].astype(F32)
+        out[...] = total.astype(BF)
+
+    summed(0, att_stage, att_recv, attended)
+    summed(1, tok_stage, tok_recv, token_grad)
+    summed(2, lat_stage, lat_recv, latent_grad)
+
+    for k in range(1, n_seq):
+        peer = zp(k)
+        for make in (q_copy, g_copy, acc_copy, st_copy, norm_copy, dq_copy):
+            make(peer, z).wait_send()
+    for copy in (k_copy, v_copy, b_copy, dkv_copy):
+        copy.wait_send()
+    for k in range(1, n_head):
+        h_copy(0, att_stage, att_recv, hp(k), h).wait_send()
+        h_copy(1, tok_stage, tok_recv, hp(k), h).wait_send()
+        h_copy(2, lat_stage, lat_recv, hp(k), h).wait_send()
+
+
+def fused(n_seq, n_head, n_rep, latents, cotangent, tokens, counts, w_query, w_key, w_value, w_out):
+    lat, tok, cols = latents.shape[0], tokens.shape[0], w_query.shape[1]
+    wide = 2 * D // HEADS
+    pairs = cols // wide
+    vmem = pltpu.VMEM
+    dma = pltpu.SemaphoreType.DMA
+    stats = vmem((n_seq, pairs, 2, 2 * lat), F32)
+    block = vmem((n_seq, cols, lat), BF)
+    scratch = [
+        vmem((n_seq, lat, cols), BF),
+        vmem((n_seq, lat, cols), BF),
+        vmem((cols, lat), BF),
+        vmem((2 * tok, cols), BF),
+        vmem((2 * tok, cols), BF),
+        vmem((cols, 2 * tok), BF),
+        vmem((cols, 2 * tok), BF),
+        vmem((2 * tok, 128), F32),
+        vmem((n_seq, pairs, 2 * tok, 2 * lat), F32),
+        vmem((n_seq, pairs, 1, 2 * lat), F32),
+        block,
+        block,
+        stats,
+        stats,
+        stats,
+        block,
+        block,
+        vmem((2 * tok, cols), F32),
+        vmem((2 * tok, cols), F32),
+        vmem((2, tok, cols), BF),
+        vmem((2, tok, cols), BF),
+        vmem((n_head, lat, cols), BF),
+        vmem((n_head, lat, cols), BF),
+        vmem((n_head, lat, cols), BF),
+        vmem((n_head, lat, cols), BF),
+        vmem((n_head, tok, cols), BF),
+        vmem((n_head, tok, cols), BF),
+        dma((6, n_seq)),
+        dma((6, n_seq)),
+        dma((4,)),
+        dma((4,)),
+        dma((3, n_head)),
+        dma((3, n_head)),
+    ]
+    whole = pl.BlockSpec(memory_space=pltpu.VMEM)
+    return pl.pallas_call(
+        functools.partial(fused_kernel, n_seq, n_head, n_rep),
+        out_shape=(
+            jax.ShapeDtypeStruct((lat, cols), BF),
+            jax.ShapeDtypeStruct((lat, cols), BF),
+            jax.ShapeDtypeStruct((tok, cols), BF),
+        ),
+        in_specs=[whole] * 3 + [pl.BlockSpec(memory_space=pltpu.SMEM)] + [whole] * 4,
+        out_specs=(whole,) * 3,
+        scratch_shapes=scratch,
+        compiler_params=pltpu.CompilerParams(
+            collective_id=0, has_side_effects=True, vmem_limit_bytes=48 * 1024 * 1024
+        ),
+    )(latents, cotangent, tokens, counts, w_query, w_key, w_value, w_out)
+
+
 def solution(mesh):
     in_specs = (
         P(("grp", "seq", "rep"), None),
@@ -152,6 +462,13 @@
         P(("grp", "seq", "rep"), "head"),
         P(("grp", "seq", "rep"), "head"),
     )
+    n_seq, n_head, n_rep = mesh.shape["seq"], mesh.shape["head"], mesh.shape["rep"]
+
+    def body(*operands):
+        if operands[0].shape[0] % 128 == 0 and n_rep == 2:
+            return fused(n_seq, n_head, n_rep, *operands)
+        return on_device(*operands)
+
     return jax.shard_map(
-        on_device, mesh=mesh, in_specs=in_specs, out_specs=out_specs, check_vma=False
-    )
+        body, mesh=mesh, in_specs=in_specs, out_specs=out_specs, check_vma=False
+    )

time: 513 us -> 72.4 us (0.14)
  waiting for transfers between devices: 178 us -> 0 us
  blocking collectives: 93.3 us -> 0 us
  matrix products: 90.3 us -> 0 us
  local copies, waits for them, and re-layouts: 83.2 us -> 9.85 us
  Pallas kernels: 0 us -> 60.5 us
  other arithmetic: 48.5 us -> 0 us
  between operations: 14.3 us -> 1.3 us
    all_gather x3 -> x0, waiting for transfers between devices: 139 us -> none  [the longest x1 119 us: combined_all(): pieces = jax.tree.map(lambda part: lax.all_gather(part, axis), value)]
    dot_general x64 -> x0, matrix products: 90.3 us -> none  [the longest x28 37.8 us: contract_last(): lax.dot_general(left, right, (((1,), (1,)), ((), ())), preferred_element_...]
    psum x1 -> x0, blocking collectives: 62.7 us -> none  [on_device(): query_total = lax.psum(query_terms, ('seq', 'rep'))]
    pallas_call x0 -> x1, Pallas kernels: none -> 60.5 us  [fused(): pl.pallas_call(functools.partial(fused_kernel, n_seq, n_head, n_rep), out...]
    dynamic_slice x22 -> x0, local copies, waits for them, and re-layouts: 41.3 us -> none  [the longest x14 35.1 us: combined_all(): lax.scan(lambda running, slab: (join(running, slab), None), head, tail)]
    reduce_scatter x3 -> x0, waiting for transfers between devices: 39.5 us -> none  [the longest x1 17.3 us: on_device(): lax.psum_scatter(token_terms.astype(jnp.bfloat16), 'head', scatter_dimens...]
    all_gather x2 -> x0, blocking collectives: 30.6 us -> none  [combined_all(): pieces = jax.tree.map(lambda part: lax.all_gather(part, axis), value)]
    add x14 -> x0, other arithmetic: 29.4 us -> none  [the longest x7 23.9 us: merge_parts(): accum_first * jnp.repeat(factor_first, repeats, axis=-1)]
  transfers between devices with their start and end apart: 6 -> 0, of which waited for: 5 -> 0; matrix products, arithmetic and copies ran while one was open for 11% -> 0% of each run, Pallas kernels for 0% -> 0%
where the time goes in v1:
time: 72.4 us; the launch traced here: 71.6 us
  Pallas kernels  60.5 us (84%)
  local copies, waits for them, and re-layouts  9.85 us (14%)
  between operations  1.3 us (2%)
    pallas_call x1, Pallas kernels, fused(): pl.pallas_call(functools.partial(fused_kernel, n_seq, n_head, n_rep), out...  60.5 us
    unnamed x17, local copies, waits for them, and re-layouts  9.85 us

profile of v1, /device:TPU:0, one launch (start us, length us, event | category | flops | bytes accessed | tf_op | source)
XLA Modules:
  0.0 71.6 jit_solution(1141919134343136004)
XLA Ops:
  1.3 0.0 copy-start
  1.3 1.2 %copy-done = bf16[1024,512]{1,0:T(8,128)(2,1)S(1)} copy-done((bf16[1024,512]{1,0:T(8,128)(2,1)S(1)}, bf16[1024,512]{1,0:T(8,128)(2,1)}, u32[]{:S(2)}) %copy-start) | copy-done | bytes 1048600
  2.5 0.0 copy-start.1
  2.5 1.2 %copy-done.1 = bf16[1024,512]{1,0:T(8,128)(2,1)S(1)} copy-done((bf16[1024,512]{1,0:T(8,128)(2,1)S(1)}, bf16[1024,512]{1,0:T(8,128)(2,1)}, u32[]{:S(2)}) %copy-start.1) | copy-done | bytes 1048600
  3.7 0.0 copy-start.2
  3.7 1.2 %copy-done.2 = bf16[1024,512]{1,0:T(8,128)(2,1)S(1)} copy-done((bf16[1024,512]{1,0:T(8,128)(2,1)S(1)}, bf16[1024,512]{1,0:T(8,128)(2,1)}, u32[]{:S(2)}) %copy-start.2) | copy-done | bytes 1048600
  5.0 0.0 copy-start.3
  5.0 1.2 %copy-done.3 = bf16[512,1024]{1,0:T(8,128)(2,1)S(1)} copy-done((bf16[512,1024]{1,0:T(8,128)(2,1)S(1)}, bf16[512,1024]{1,0:T(8,128)(2,1)}, u32[]{:S(2)}) %copy-start.3) | copy-done | bytes 1048600
  6.2 0.0 copy-start.4
  6.2 1.0 %copy-done.4 = bf16[256,1024]{1,0:T(8,128)(2,1)S(1)} copy-done((bf16[256,1024]{1,0:T(8,128)(2,1)S(1)}, bf16[256,1024]{1,0:T(8,128)(2,1)}, u32[]{:S(2)}) %copy-start.4) | copy-done | bytes 524312
  7.2 0.0 copy-start.5
  7.2 0.9 %copy-done.5 = bf16[128,1024]{1,0:T(8,128)(2,1)S(1)} copy-done((bf16[128,1024]{1,0:T(8,128)(2,1)S(1)}, bf16[128,1024]{1,0:T(8,128)(2,1)}, u32[]{:S(2)}) %copy-start.5) | copy-done | bytes 262168
  8.2 0.0 copy-start.6
  8.2 0.9 %copy-done.6 = bf16[128,1024]{1,0:T(8,128)(2,1)S(1)} copy-done((bf16[128,1024]{1,0:T(8,128)(2,1)S(1)}, bf16[128,1024]{1,0:T(8,128)(2,1)}, u32[]{:S(2)}) %copy-start.6) | copy-done | bytes 262168
  9.1 60.5 %shard_map.103 = (bf16[128,512]{1,0:T(8,128)(2,1)S(1)}, bf16[128,512]{1,0:T(8,128)(2,1)S(1)}, bf16[256,512]{1,0:T(8,128)(2,1)S(1)}) custom-call(bf16[128,1024]{1,0:T(8,128)(2,1)S(1)} %copy-done.5, bf16[128,1024]{1,0:T(8,128)(2,1)S(1)} %copy-done.6, bf16[256,1024]{1,0:T(8,128)(2,1)S(1)} %copy-done.4, s32[1]{0:T(128)S(6)} %copy.14.counts, ...), custom_call_target="tpu_custom_call" | custom-call | tf_op jit(solution)/shard_map/pallas_call | solution.py:433
  69.6 0.7 copy.15
  70.3 0.7 copy.16
  70.9 0.7 copy.17
Async XLA Ops:
  1.3 1.2 %copy-start = (bf16[1024,512]{1,0:T(8,128)(2,1)S(1)}, bf16[1024,512]{1,0:T(8,128)(2,1)}, u32[]{:S(2)}) copy-start(bf16[1024,512]{1,0:T(8,128)(2,1)} %w_query.1) | copy-start | bytes 3145732
  2.5 1.2 %copy-start.1 = (bf16[1024,512]{1,0:T(8,128)(2,1)S(1)}, bf16[1024,512]{1,0:T(8,128)(2,1)}, u32[]{:S(2)}) copy-start(bf16[1024,512]{1,0:T(8,128)(2,1)} %w_key.1) | copy-start | bytes 3145732
  3.7 1.2 %copy-start.2 = (bf16[1024,512]{1,0:T(8,128)(2,1)S(1)}, bf16[1024,512]{1,0:T(8,128)(2,1)}, u32[]{:S(2)}) copy-start(bf16[1024,512]{1,0:T(8,128)(2,1)} %w_value.1) | copy-start | bytes 3145732
  5.0 1.2 %copy-start.3 = (bf16[512,1024]{1,0:T(8,128)(2,1)S(1)}, bf16[512,1024]{1,0:T(8,128)(2,1)}, u32[]{:S(2)}) copy-start(bf16[512,1024]{1,0:T(8,128)(2,1)} %w_out.1) | copy-start | bytes 3145732
  6.2 1.0 %copy-start.4 = (bf16[256,1024]{1,0:T(8,128)(2,1)S(1)}, bf16[256,1024]{1,0:T(8,128)(2,1)}, u32[]{:S(2)}) copy-start(bf16[256,1024]{1,0:T(8,128)(2,1)} %tokens.1) | copy-start | bytes 1572868
  7.2 0.9 %copy-start.5 = (bf16[128,1024]{1,0:T(8,128)(2,1)S(1)}, bf16[128,1024]{1,0:T(8,128)(2,1)}, u32[]{:S(2)}) copy-start(bf16[128,1024]{1,0:T(8,128)(2,1)} %latents.1) | copy-start | bytes 786436
  8.2 0.9 %copy-start.6 = (bf16[128,1024]{1,0:T(8,128)(2,1)S(1)}, bf16[128,1024]{1,0:T(8,128)(2,1)}, u32[]{:S(2)}) copy-start(bf16[128,1024]{1,0:T(8,128)(2,1)} %cotangent.1) | copy-start | bytes 786436

commit v2 on v1

--- a/solution.py
+++ b/solution.py
@@ -153,8 +153,9 @@
 
 def fused_kernel(
     n_seq, n_head, n_rep,
-    latents, cotangent, tokens, counts, w_query, w_key, w_value, w_out,
+    latents_in, cotangent_in, tokens_in, counts, w_query_in, w_key_in, w_value_in, w_out_in,
     attended, latent_grad, token_grad,
+    latents, cotangent, tokens, w_query, w_key, w_value, w_out, in_sem,
     q_all, g_all, g_t, k_all, v_all, k_t, v_t, bias, expo, highs,
     acc_send, acc_recv, st_send, st_recv, norm_row, dq_send, dq_recv, dk, dv, dkv_send, dkv_recv,
     att_stage, att_recv, lat_stage, lat_recv, tok_stage, tok_recv,
@@ -174,6 +175,15 @@
     def hp(k):
         return lax.rem(h + k, n_head)
 
+    loads = [
+        pltpu.make_async_copy(source, landing, in_sem.at[i])
+        for i, (source, landing) in enumerate((
+            (latents_in, latents), (w_query_in, w_query), (tokens_in, tokens), (w_key_in, w_key),
+            (w_value_in, w_value), (cotangent_in, cotangent), (w_out_in, w_out),
+        ))
+    ]
+    for load in loads:
+        load.start()
     barrier = pltpu.get_barrier_semaphore()
     for k in range(1, n_seq):
         pl.semaphore_signal(barrier, inc=1, device_id={"seq": zp(k)}, device_id_type=MESH)
@@ -184,11 +194,60 @@
     def z_copy(kind, src, dst, peer, slot_send, slot_recv):
         return remote(src, dst, z_send.at[kind, slot_send], z_recv.at[kind, slot_recv], {"seq": peer})
 
-    def q_copy(peer, owner):
-        return z_copy(0, q_all.at[owner], q_all.at[owner], peer, peer, owner)
-
-    def g_copy(peer, owner):
-        return z_copy(1, g_all.at[owner], g_all.at[owner], peer, peer, owner)
+    to_right, to_left = z + 1 < n_seq, z > 0
+
+    def line(kind, blocks):
+        def copy(owner, peer, slot):
+            return z_copy(kind, blocks.at[owner], blocks.at[owner], peer, slot, owner)
+
+        return copy
+
+    q_line, g_line = line(0, q_all), line(1, g_all)
+
+    def visit(k):
+        short = jnp.minimum(z, n_seq - 1 - z)
+        paired = k <= 2 * short
+        far = jnp.where(paired, (k + 1) // 2, k - short)
+        from_left = jnp.where(paired, lax.rem(k, 2), jnp.where(z > n_seq - 1 - z, 1, 0)) == 1
+        return jnp.where(from_left, z - far, z + far), from_left
+
+    def send_own(copy):
+        @pl.when(to_right)
+        def _():
+            copy(z, z + 1, z).start()
+
+        @pl.when(to_left)
+        def _():
+            copy(z, z - 1, n_seq).start()
+
+    def own_sent(copy):
+        @pl.when(to_right)
+        def _():
+            copy(z, z + 1, z).wait_send()
+
+        @pl.when(to_left)
+        def _():
+            copy(z, z - 1, n_seq).wait_send()
+
+    def pass_on(copy, j, from_left):
+        copy(j, j, j).wait_recv()
+
+        @pl.when(jnp.logical_and(from_left, to_right))
+        def _():
+            copy(j, z + 1, j).start()
+
+        @pl.when(jnp.logical_and(jnp.logical_not(from_left), to_left))
+        def _():
+            copy(j, z - 1, j).start()
+
+    def passed(copy, j, from_left):
+        @pl.when(jnp.logical_and(from_left, to_right))
+        def _():
+            copy(j, z + 1, j).wait_send()
+
+        @pl.when(jnp.logical_and(jnp.logical_not(from_left), to_left))
+        def _():
+            copy(j, z - 1, j).wait_send()
 
     def acc_copy(peer, sender):
         return z_copy(2, acc_send.at[peer], acc_recv.at[sender], peer, peer, sender)
@@ -216,21 +275,26 @@
             stage.at[peer], landing.at[sender], h_send.at[index, peer], h_recv.at[index, sender], {"head": peer}
         )
 
+    loads[0].wait()
+    loads[1].wait()
     q_all[z] = (jnp.dot(latents[...], w_query[...], preferred_element_type=F32).astype(BF) * scale).astype(BF)
     pl.semaphore_wait(barrier, n_seq - 1 + n_head - 1 + 1)
-    for k in range(1, n_seq):
-        q_copy(zp(k), z).start()
+    send_own(q_line)
+    loads[2].wait()
+    loads[3].wait()
     k_all[own, :] = jnp.dot(tokens[...], w_key[...], preferred_element_type=F32).astype(BF)
     k_copy.start()
     rows = lax.broadcasted_iota(jnp.int32, (tok, 128), 0)
     bias[own, :] = jnp.where(rows < counts[0], 0.0, -jnp.inf).astype(F32)
     b_copy.start()
+    loads[4].wait()
     v_all[own, :] = jnp.dot(tokens[...], w_value[...], preferred_element_type=F32).astype(BF)
     v_copy.start()
+    loads[5].wait()
+    loads[6].wait()
     grads = contract_last(cotangent[...], w_out[...])
     g_all[z] = grads.astype(BF)
-    for k in range(1, n_seq):
-        g_copy(zp(k), z).start()
+    send_own(g_line)
     g_t[...] = grads.T.astype(BF)
     k_t[:, 0:tok] = k_all[own, :].astype(F32).T.astype(BF)
     v_t[:, 0:tok] = v_all[own, :].astype(F32).T.astype(BF)
@@ -269,11 +333,12 @@
     forward(z, acc_recv.at[z], st_recv.at[z])
 
     def forward_step(k, carry):
-        j = zp(k)
-        q_copy(j, j).wait_recv()
+        j, from_left = visit(k)
+        pass_on(q_line, j, from_left)
         forward(j, acc_send.at[j], st_send.at[j])
         acc_copy(j, z).start()
         st_copy(j, z).start()
+        pass_on(g_line, j, from_left)
         return carry
 
     lax.fori_loop(1, n_seq, forward_step, 0)
@@ -334,8 +399,7 @@
     backward(z, dq_recv.at[z])
 
     def backward_step(k, carry):
-        j = zp(k)
-        g_copy(j, j).wait_recv()
+        j, _ = visit(k)
         norm_copy(j, j).wait_recv()
         backward(j, dq_send.at[j])
         dq_copy(j, z).start()
@@ -376,8 +440,18 @@
 
     for k in range(1, n_seq):
         peer = zp(k)
-        for make in (q_copy, g_copy, acc_copy, st_copy, norm_copy, dq_copy):
+        for make in (acc_copy, st_copy, norm_copy, dq_copy):
             make(peer, z).wait_send()
+
+    def drain(k, carry):
+        j, from_left = visit(k)
+        passed(q_line, j, from_left)
+        passed(g_line, j, from_left)
+        return carry
+
+    lax.fori_loop(1, n_seq, drain, 0)
+    own_sent(q_line)
+    own_sent(g_line)
     for copy in (k_copy, v_copy, b_copy, dkv_copy):
         copy.wait_send()
     for k in range(1, n_head):
@@ -394,7 +468,9 @@
     dma = pltpu.SemaphoreType.DMA
     stats = vmem((n_seq, pairs, 2, 2 * lat), F32)
     block = vmem((n_seq, cols, lat), BF)
-    scratch = [
+    held = [latents, cotangent, tokens, w_query, w_key, w_value, w_out]
+    scratch = [vmem(array.shape, array.dtype) for array in held] + [
+        dma((7,)),
         vmem((n_seq, lat, cols), BF),
         vmem((n_seq, lat, cols), BF),
         vmem((cols, lat), BF),
@@ -422,7 +498,7 @@
         vmem((n_head, lat, cols), BF),
         vmem((n_head, tok, cols), BF),
         vmem((n_head, tok, cols), BF),
-        dma((6, n_seq)),
+        dma((6, n_seq + 1)),
         dma((6, n_seq)),
         dma((4,)),
         dma((4,)),
@@ -430,6 +506,7 @@
         dma((3, n_head)),
     ]
     whole = pl.BlockSpec(memory_space=pltpu.VMEM)
+    far = pl.BlockSpec(memory_space=pl.ANY)
     return pl.pallas_call(
         functools.partial(fused_kernel, n_seq, n_head, n_rep),
         out_shape=(
@@ -437,11 +514,11 @@
             jax.ShapeDtypeStruct((lat, cols), BF),
             jax.ShapeDtypeStruct((tok, cols), BF),
         ),
-        in_specs=[whole] * 3 + [pl.BlockSpec(memory_space=pltpu.SMEM)] + [whole] * 4,
+        in_specs=[far] * 3 + [pl.BlockSpec(memory_space=pltpu.SMEM)] + [far] * 4,
         out_specs=(whole,) * 3,
         scratch_shapes=scratch,
         compiler_params=pltpu.CompilerParams(
-            collective_id=0, has_side_effects=True, vmem_limit_bytes=48 * 1024 * 1024
+            collective_id=0, has_side_effects=True, vmem_limit_bytes=56 * 1024 * 1024
         ),
     )(latents, cotangent, tokens, counts, w_query, w_key, w_value, w_out)
 

time: 72.4 us -> 62.5 us (0.86)
  local copies, waits for them, and re-layouts: 9.85 us -> 2.98 us
  Pallas kernels: 60.5 us -> 58 us
    unnamed x17 -> x7, local copies, waits for them, and re-layouts: 9.85 us -> 2.98 us
    pallas_call x1, Pallas kernels: 60.5 us -> 58 us  [fused(): pl.pallas_call(functools.partial(fused_kernel, n_seq, n_head, n_rep), out...]
where the time goes in v2:
time: 62.5 us; the launch traced here: 62.3 us
  Pallas kernels  58 us (93%)
  local copies, waits for them, and re-layouts  2.98 us (5%)
  between operations  1.3 us (2%)
    pallas_call x1, Pallas kernels, fused(): pl.pallas_call(functools.partial(fused_kernel, n_seq, n_head, n_rep), out...  58 us
    unnamed x7, local copies, waits for them, and re-layouts  2.98 us

profile of v2, /device:TPU:0, one launch (start us, length us, event | category | flops | bytes accessed | tf_op | source)
XLA Modules:
  0.0 62.3 jit_solution(2614519441254120229)
XLA Ops:
  1.3 58.0 %shard_map.103 = (bf16[128,512]{1,0:T(8,128)(2,1)}, bf16[128,512]{1,0:T(8,128)(2,1)}, bf16[256,512]{1,0:T(8,128)(2,1)}) custom-call(bf16[128,1024]{1,0:T(8,128)(2,1)} %latents_in.1, bf16[128,1024]{1,0:T(8,128)(2,1)} %cotangent_in.1, bf16[256,1024]{1,0:T(8,128)(2,1)} %tokens_in.1, s32[1]{0:T(128)S(6)} %copy.14.counts, bf16[1024,512]{1,0:T(8,128)(2,1)} %w_query_in.1, ...), custom_call_target="tpu_custom_call" | custom-call | tf_op jit(solution)/shard_map/pallas_call | solution.py:510
  59.3 0.0 copy-start.1
  59.3 0.0 copy-start
  59.3 1.6 %copy.15 = bf16[128,512]{1,0:T(8,128)(2,1)} copy(bf16[128,512]{1,0:T(8,128)(2,1)} %get-tuple-element.6) | data formatting | bytes 262144
  61.0 0.0 copy-done.1
  61.0 0.7 %copy.16 = bf16[128,512]{1,0:T(8,128)(2,1)} copy(bf16[128,512]{1,0:T(8,128)(2,1)S(1)} %copy-done.1) | data formatting | bytes 262144
  61.6 0.0 copy-done
  61.6 0.7 %copy.17 = bf16[256,512]{1,0:T(8,128)(2,1)} copy(bf16[256,512]{1,0:T(8,128)(2,1)S(1)} %copy-done) | data formatting | bytes 524288
Async XLA Ops:
  59.3 1.6 %copy-start.1 = (bf16[128,512]{1,0:T(8,128)(2,1)S(1)}, bf16[128,512]{1,0:T(8,128)(2,1)}, u32[]{:S(2)}) copy-start(bf16[128,512]{1,0:T(8,128)(2,1)} %get-tuple-element.7) | copy-start | bytes 393220
  59.3 2.3 %copy-start = (bf16[256,512]{1,0:T(8,128)(2,1)S(1)}, bf16[256,512]{1,0:T(8,128)(2,1)}, u32[]{:S(2)}) copy-start(bf16[256,512]{1,0:T(8,128)(2,1)} %get-tuple-element.8) | copy-start | bytes 786436
